TPU v7x, 512 devices: a whole 4x8x8 slice. The times are simulated.
512 devices in a mesh: dp: 512 (over z, x, y, core).
Axes of the slice: x: 4, y: 8, z: 8, core: 2. Of those that a mesh axis runs over, the one named last changes fastest.
Arguments:
- image: bfloat16 [65536, 1152], P('dp')
- text: bfloat16 [65536, 1152], P('dp')
- plan: int32 [5, 512], replicated, may hold values from 0 to 511, as said below
- offset: int32 [1], replicated, may hold values from 0 to 2
- logit_scale: float32 [1], replicated, may hold values from 16 to 64
- logit_bias: float32 [1], replicated, may hold values from -3 to 0
Outputs:
- row_loss: float32 [65536], P('dp')
- image_grad: float32 [65536, 1152], P('dp')
- text_grad: float32 [65536, 1152], P('dp')
Inputs may be any that keep to these rules, and one draw needn't show every extreme that they name: `plan`: in every row r there is a bit b_r, different in each row, such that device p's partner is p XOR 2 ** b_r; in row 2 that bit is the highest one, so the partner is half the devices away.
All inputs are finite; a program needn't handle non-finite values.
Results may differ from a plain program's by a relative error of at most 0.0057.
Values may be sent and summed in bfloat16 or wider, within the bound.
A program may use at most 64 MiB of HBM per device.

v0:
```python
from functools import partial

import jax
import jax.numpy as jnp
from jax import lax
from jax.sharding import PartitionSpec as P

ROUNDS = 3


def as_sent(array):
    return jax.tree.map(lambda a: a.astype(jnp.bfloat16) if a.dtype == jnp.float32 else a, array)


def partner_2(value, axis, distance):
    mask = 2**distance
    pairs = [(source, source ^ mask) for source in range(lax.axis_size(axis))]
    return lax.ppermute(value, axis, pairs)


def unit_rows(values):
    whole = values.astype(jnp.float32)
    norms = jnp.sqrt(jnp.sum(whole * whole, axis=-1, keepdims=True) + 1e-06)
    return (whole / norms, norms)


def finish(direction, unit_exact, norms):
    inner = jnp.sum(unit_exact * direction, axis=-1, keepdims=True)
    return (direction - unit_exact * inner) / norms


def text_step(values, bit):
    return jax.tree.map(
        lambda part, own: part.astype(own.dtype), partner_2(as_sent(values), "dp", bit), values
    )


def terms_step(values, bit):
    return jax.tree.map(
        lambda part, own: part.astype(own.dtype), partner_2(as_sent(values), "dp", bit), values
    )


def move_by(step_fn, values, bit_index):
    bit_count = lax.axis_size("dp").bit_length() - 1
    branches = [partial(step_fn, bit=k) for k in range(bit_count)]
    return lax.switch(bit_index, branches, values)


def pair_block(img_block, txt_block, labels, scale_val, bias_val):
    logits = (
        scale_val * jnp.dot(img_block, txt_block.T, preferred_element_type=jnp.float32) + bias_val
    )
    coef = (-labels * jax.nn.sigmoid(-labels * logits)).astype(jnp.bfloat16)
    losses = jnp.sum(jax.nn.softplus(-labels * logits), axis=-1)
    img_part = scale_val * jnp.dot(coef, txt_block, preferred_element_type=jnp.float32)
    return (coef, losses, img_part)


def text_part(coef, img_block, scale_val):
    return scale_val * jnp.einsum("ij,id->jd", coef, img_block, preferred_element_type=jnp.float32)


def per_device(image, text, plan, offset, logit_scale, logit_bias):
    my_index = lax.axis_index("dp")
    bit_count = lax.axis_size("dp").bit_length() - 1
    img_exact, img_norm = unit_rows(image)
    txt_exact, txt_norm = unit_rows(text)
    img_unit = img_exact.astype(jnp.bfloat16)
    txt_unit = txt_exact.astype(jnp.bfloat16)
    scale_val = logit_scale[0]
    bias_val = logit_bias[0]
    row_count = image.shape[0]
    labels = 2.0 * jnp.eye(row_count, dtype=jnp.float32) - 1.0
    coef, losses, img_dir = pair_block(img_unit, txt_unit, labels, scale_val, bias_val)
    txt_dir = text_part(coef, img_unit, scale_val)
    bit_values = jnp.arange(bit_count, dtype=jnp.int32)
    for round_idx in range(ROUNDS):
        partner_row = lax.dynamic_index_in_dim(plan, offset[0] + round_idx, 0, keepdims=False)
        partner = lax.dynamic_index_in_dim(partner_row, my_index, 0, keepdims=False)
        flipped = jnp.bitwise_xor(partner, my_index)
        powers = jnp.left_shift(jnp.ones_like(bit_values), bit_values)
        bit_index = jnp.sum(jnp.where(powers == flipped, bit_values, 0))
        txt_other = move_by(text_step, txt_unit, bit_index)
        img_other = None
        bit_index, txt_other, img_other = (bit_index, txt_other, img_other)
        coef, more_loss, img_part = pair_block(
            img_unit, txt_other, jnp.float32(-1.0), scale_val, bias_val
        )
        txt_term = text_part(coef, img_unit, scale_val).astype(jnp.bfloat16)
        txt_back = move_by(terms_step, txt_term, bit_index)
        txt_dir = txt_dir + txt_back.astype(jnp.float32)
        losses = losses + more_loss
        img_dir = img_dir + img_part
    image_grad = finish(img_dir, img_exact, img_norm)
    text_grad = finish(txt_dir, txt_exact, txt_norm)
    return (losses, image_grad, text_grad)


def solution(mesh):
    in_specs = (P("dp", None), P("dp", None), P(), P(), P(), P())
    out_specs = (P("dp"), P("dp", None), P("dp", None))
    return jax.shard_map(
        per_device, mesh=mesh, in_specs=in_specs, out_specs=out_specs, check_vma=False
    )
```

profile of v0, /device:TPU:198, one launch (start us, length us, event | category | flops | bytes accessed | tf_op | source)
XLA Modules:
  0.0 103.3 jit_solution(10012068560234605031)
XLA Ops:
  3.6 1.5 %fusion.24 = (s32[1,1]{1,0:T(1,128)}, s32[1,1]{1,0:T(1,128)}, s32[1,1]{1,0:T(1,128)}) fusion(s32[5,512]{1,0:T(8,128)} %param.62, s32[]{:T(128)S(6)} %select_n.49, s32[]{:T(128)S(6)} %select_n.51, s32[]{:T(128)S(6)} %select_n.59, s32[]{:T(128)S(6)} %select_n.55), kind=kLoop, calls=%fused_computation.60 | loop fusion | bytes 40 | tf_op jit(solution)/shard_map/jit(dynamic_index_in_dim)/dynamic_slice | solution.py:80
  7.0 10.8 %conditional.17 = (bf16[128,1152]{1,0:T(8,128)(2,1)}) conditional(s32[]{:T(128)} %clamp.26, bf16[128,1152]{1,0:T(8,128)(2,1)S(1)} %get-tuple-element.151, bf16[128,1152]{1,0:T(8,128)(2,1)S(1)} %get-tuple-element.151, bf16[128,1152]{1,0:T(8,128)(2,1)S(1)} %get-tuple-element.151, ...), branch_computations={%region_26.27_spmd, %region_27.28_spmd, %region_28.29_spmd, %regio... | conditional | bytes 1179696 | solution.py:47
  7.0 1.9 %collective-permute-start.24 = (bf16[128,1152]{1,0:T(8,128)(2,1)S(1)}, bf16[128,1152]{1,0:T(8,128)(2,1)}, u32[]{:S(2)}, u32[]{:S(2)}) collective-permute-start(bf16[128,1152]{1,0:T(8,128)(2,1)S(1)} %param.24), channel_id=1, source_target_pairs={{0,64},{1,65},{2,66},{3,67},{4,68},{5,69},{6,70},{7,71},{8,72},{9,... | collective-permute-start | bytes 884744 | tf_op jit(solution)/shard_map/cond/branch_6_fun/ppermute | solution.py:18
  8.9 8.8 %collective-permute-done.24 = bf16[128,1152]{1,0:T(8,128)(2,1)} collective-permute-done((bf16[128,1152]{1,0:T(8,128)(2,1)S(1)}, bf16[128,1152]{1,0:T(8,128)(2,1)}, u32[]{:S(2)}, u32[]{:S(2)}) %collective-permute-start.24) | collective-permute-done | bytes 294944 | tf_op jit(solution)/shard_map/cond/branch_6_fun/ppermute | solution.py:18
  18.4 1.3 %fusion.17 = (f32[128]{0:T(128)S(1)}, f32[128,128]{0,1:T(8,128)S(1)}) fusion(f32[]{:T(128)} %bitcast.39, bf16[128,1152]{1,0:T(8,128)(2,1)S(1)} %get-tuple-element.150, bf16[128,1152]{1,0:T(8,128)(2,1)} %get-tuple-element.154, f32[]{:T(128)} %bitcast.35), kind=kOutput, calls=%fused_computation.40 | convolution fusion | flops 37896064 | bytes 655880 | tf_op jit(solution)/shard_map/dot_general | solution.py:52
  21.6 9.9 %conditional.16 = (bf16[128,1152]{1,0:T(8,128)(2,1)}) conditional(s32[]{:T(128)} %clamp.25, bf16[128,1152]{1,0:T(8,128)(2,1)S(1)} %get-tuple-element.151, bf16[128,1152]{1,0:T(8,128)(2,1)S(1)} %get-tuple-element.151, bf16[128,1152]{1,0:T(8,128)(2,1)S(1)} %get-tuple-element.151, ...), branch_computations={%region_15.16_spmd, %region_16.17_spmd, %region_17.18_spmd, %regio... | conditional | bytes 1179696 | solution.py:47
  21.7 2.7 %collective-permute-start.13 = (bf16[128,1152]{1,0:T(8,128)(2,1)S(1)}, bf16[128,1152]{1,0:T(8,128)(2,1)}, u32[]{:S(2)}, u32[]{:S(2)}) collective-permute-start(bf16[128,1152]{1,0:T(8,128)(2,1)S(1)} %param.13), channel_id=1, source_target_pairs={{0,16},{1,17},{2,18},{3,19},{4,20},{5,21},{6,22},{7,23},{8,24},{9,... | collective-permute-start | bytes 884744 | tf_op jit(solution)/shard_map/cond/branch_4_fun/ppermute | solution.py:18
  24.4 7.1 %collective-permute-done.13 = bf16[128,1152]{1,0:T(8,128)(2,1)} collective-permute-done((bf16[128,1152]{1,0:T(8,128)(2,1)S(1)}, bf16[128,1152]{1,0:T(8,128)(2,1)}, u32[]{:S(2)}, u32[]{:S(2)}) %collective-permute-start.13) | collective-permute-done | bytes 294944 | tf_op jit(solution)/shard_map/cond/branch_4_fun/ppermute | solution.py:18
  31.6 1.3 %fusion.16 = (f32[128]{0:T(128)S(1)}, f32[128,128]{0,1:T(8,128)S(1)}) fusion(f32[]{:T(128)} %bitcast.40, bf16[128,1152]{1,0:T(8,128)(2,1)S(1)} %get-tuple-element.150, bf16[128,1152]{1,0:T(8,128)(2,1)} %get-tuple-element.153, f32[]{:T(128)} %bitcast.36), kind=kOutput, calls=%fused_computation.39 | convolution fusion | flops 37896064 | bytes 655880 | tf_op jit(solution)/shard_map/dot_general | solution.py:52
  35.1 15.6 %conditional.15 = (bf16[128,1152]{1,0:T(8,128)(2,1)}) conditional(s32[]{:T(128)} %clamp.24, bf16[128,1152]{1,0:T(8,128)(2,1)S(1)} %get-tuple-element.151, bf16[128,1152]{1,0:T(8,128)(2,1)S(1)} %get-tuple-element.151, bf16[128,1152]{1,0:T(8,128)(2,1)S(1)} %get-tuple-element.151, ...), branch_computations={%region_4.5_spmd, %region_5.6_spmd, %region_6.7_spmd, %region_7.8_... | conditional | bytes 1179696 | solution.py:47
  35.1 8.2 %collective-permute-start.8 = (bf16[128,1152]{1,0:T(8,128)(2,1)S(1)}, bf16[128,1152]{1,0:T(8,128)(2,1)}, u32[]{:S(2)}, u32[]{:S(2)}) collective-permute-start(bf16[128,1152]{1,0:T(8,128)(2,1)S(1)} %param.8), channel_id=1, source_target_pairs={{0,256},{1,257},{2,258},{3,259},{4,260},{5,261},{6,262},{7,263},{8... | collective-permute-start | bytes 884744 | tf_op jit(solution)/shard_map/cond/branch_8_fun/ppermute | solution.py:18
  43.3 7.4 %collective-permute-done.8 = bf16[128,1152]{1,0:T(8,128)(2,1)} collective-permute-done((bf16[128,1152]{1,0:T(8,128)(2,1)S(1)}, bf16[128,1152]{1,0:T(8,128)(2,1)}, u32[]{:S(2)}, u32[]{:S(2)}) %collective-permute-start.8) | collective-permute-done | bytes 294944 | tf_op jit(solution)/shard_map/cond/branch_8_fun/ppermute | solution.py:18
  50.7 1.3 %fusion.15 = (f32[128]{0:T(128)S(1)}, f32[128,128]{0,1:T(8,128)S(1)}) fusion(f32[]{:T(128)} %bitcast.41, bf16[128,1152]{1,0:T(8,128)(2,1)S(1)} %get-tuple-element.150, bf16[128,1152]{1,0:T(8,128)(2,1)} %get-tuple-element.152, f32[]{:T(128)} %bitcast.37), kind=kOutput, calls=%fused_computation.38 | convolution fusion | flops 37896064 | bytes 655880 | tf_op jit(solution)/shard_map/dot_general | solution.py:52
  55.2 1.4 %multiply_reduce_fusion.1 = (f32[128]{0:T(128)S(1)}, f32[128,1152]{1,0:T(8,128)S(1)}) fusion(f32[128]{0:T(128)S(1)} %add_sqrt_fusion.1, bf16[128,1152]{1,0:T(8,128)(2,1)S(1)} %copy-done, f32[]{:T(128)} %bitcast.30, f32[128,1152]{1,0:T(8,128)S(1)} %convolution_add_fusion.1, bf16[128,1152]{1,0:T(8,128)(2,1)} %get-tuple-element.154, ...), kind=kOutput, calls=%fused_computation.32 | convolution fusion | flops 38698880 | bytes 1836036 | tf_op jit(solution)/shard_map/dot_general | solution.py:56
  57.9 14.0 %conditional.20 = (bf16[128,1152]{1,0:T(8,128)(2,1)}) conditional(s32[]{:T(128)} %clamp.26, bf16[128,1152]{1,0:T(8,128)(2,1)S(1)} %fusion.6, bf16[128,1152]{1,0:T(8,128)(2,1)S(1)} %fusion.6, bf16[128,1152]{1,0:T(8,128)(2,1)S(1)} %fusion.6, bf16[128,1152]{1,0:T(8,128)(2,1)S(1)} %fusion.6, ...), branch_computations={%region_55.56_spmd, %region_56.57_spmd, %region_57.58_spmd, %regio... | conditional | bytes 1179696
  57.9 6.8 %collective-permute-start.51 = (bf16[128,1152]{1,0:T(8,128)(2,1)S(1)}, bf16[128,1152]{1,0:T(8,128)(2,1)}, u32[]{:S(2)}, u32[]{:S(2)}) collective-permute-start(bf16[128,1152]{1,0:T(8,128)(2,1)S(1)} %param.51), channel_id=1, source_target_pairs={{0,64},{1,65},{2,66},{3,67},{4,68},{5,69},{6,70},{7,71},{8,72},{9,... | collective-permute-start | bytes 884744 | tf_op jit(solution)/shard_map/cond/branch_6_fun/ppermute | solution.py:18
  64.7 7.2 %collective-permute-done.51 = bf16[128,1152]{1,0:T(8,128)(2,1)} collective-permute-done((bf16[128,1152]{1,0:T(8,128)(2,1)S(1)}, bf16[128,1152]{1,0:T(8,128)(2,1)}, u32[]{:S(2)}, u32[]{:S(2)}) %collective-permute-start.51) | collective-permute-done | bytes 294944 | tf_op jit(solution)/shard_map/cond/branch_6_fun/ppermute | solution.py:18
  72.1 10.3 %conditional.19 = (bf16[128,1152]{1,0:T(8,128)(2,1)}) conditional(s32[]{:T(128)} %clamp.25, bf16[128,1152]{1,0:T(8,128)(2,1)S(1)} %fusion.5, bf16[128,1152]{1,0:T(8,128)(2,1)S(1)} %fusion.5, bf16[128,1152]{1,0:T(8,128)(2,1)S(1)} %fusion.5, bf16[128,1152]{1,0:T(8,128)(2,1)S(1)} %fusion.5, ...), branch_computations={%region_46.47_spmd, %region_47.48_spmd, %region_48.49_spmd, %regio... | conditional | bytes 1179696
  72.1 2.7 %collective-permute-start.40 = (bf16[128,1152]{1,0:T(8,128)(2,1)S(1)}, bf16[128,1152]{1,0:T(8,128)(2,1)}, u32[]{:S(2)}, u32[]{:S(2)}) collective-permute-start(bf16[128,1152]{1,0:T(8,128)(2,1)S(1)} %param.40), channel_id=1, source_target_pairs={{0,16},{1,17},{2,18},{3,19},{4,20},{5,21},{6,22},{7,23},{8,24},{9,... | collective-permute-start | bytes 884744 | tf_op jit(solution)/shard_map/cond/branch_4_fun/ppermute | solution.py:18
  74.9 7.6 %collective-permute-done.40 = bf16[128,1152]{1,0:T(8,128)(2,1)} collective-permute-done((bf16[128,1152]{1,0:T(8,128)(2,1)S(1)}, bf16[128,1152]{1,0:T(8,128)(2,1)}, u32[]{:S(2)}, u32[]{:S(2)}) %collective-permute-start.40) | collective-permute-done | bytes 294944 | tf_op jit(solution)/shard_map/cond/branch_4_fun/ppermute | solution.py:18
  82.7 18.0 %conditional.18 = (bf16[128,1152]{1,0:T(8,128)(2,1)}) conditional(s32[]{:T(128)} %clamp.24, bf16[128,1152]{1,0:T(8,128)(2,1)S(1)} %fusion.4, bf16[128,1152]{1,0:T(8,128)(2,1)S(1)} %fusion.4, bf16[128,1152]{1,0:T(8,128)(2,1)S(1)} %fusion.4, bf16[128,1152]{1,0:T(8,128)(2,1)S(1)} %fusion.4, ...), branch_computations={%region_37.38_spmd, %region_38.39_spmd, %region_39.40_spmd, %regio... | conditional | bytes 1179696
  82.7 7.4 %collective-permute-start.35 = (bf16[128,1152]{1,0:T(8,128)(2,1)S(1)}, bf16[128,1152]{1,0:T(8,128)(2,1)}, u32[]{:S(2)}, u32[]{:S(2)}) collective-permute-start(bf16[128,1152]{1,0:T(8,128)(2,1)S(1)} %param.35), channel_id=1, source_target_pairs={{0,256},{1,257},{2,258},{3,259},{4,260},{5,261},{6,262},{7,263},{8... | collective-permute-start | bytes 884744 | tf_op jit(solution)/shard_map/cond/branch_8_fun/ppermute | solution.py:18
  90.1 10.6 %collective-permute-done.35 = bf16[128,1152]{1,0:T(8,128)(2,1)} collective-permute-done((bf16[128,1152]{1,0:T(8,128)(2,1)S(1)}, bf16[128,1152]{1,0:T(8,128)(2,1)}, u32[]{:S(2)}, u32[]{:S(2)}) %collective-permute-start.35) | collective-permute-done | bytes 294944 | tf_op jit(solution)/shard_map/cond/branch_8_fun/ppermute | solution.py:18
  100.7 1.6 %multiply_reduce_fusion = (f32[128]{0:T(128)S(1)}, f32[128,1152]{1,0:T(8,128)S(1)}) fusion(f32[128]{0:T(128)S(1)} %add_sqrt_fusion, bf16[128,1152]{1,0:T(8,128)(2,1)S(1)} %copy-done.1, bf16[128,1152]{1,0:T(8,128)(2,1)} %get-tuple-element.157, bf16[128,1152]{1,0:T(8,128)(2,1)} %get-tuple-element.156, bf16[128,1152]{1,0:T(8,128)(2,1)} %get-tuple-element.155, ...), kind=kOutput, calls=%fused_computation.30 | convolution fusion | flops 39518080 | bytes 2130948 | tf_op jit(solution)/shard_map/ij,id->jd/dot_general | solution.py:61
  (22 shorter events, 9.8 us)
Async XLA Ops:
  0.6 1.9 %copy-start.1 = (bf16[128,1152]{1,0:T(8,128)(2,1)S(1)}, bf16[128,1152]{1,0:T(8,128)(2,1)}, u32[]{:S(2)}) copy-start(bf16[128,1152]{1,0:T(8,128)(2,1)} %param.61) | copy-start | bytes 884740
  1.3 1.3 %copy-start = (bf16[128,1152]{1,0:T(8,128)(2,1)S(1)}, bf16[128,1152]{1,0:T(8,128)(2,1)}, u32[]{:S(2)}) copy-start(bf16[128,1152]{1,0:T(8,128)(2,1)} %param.60) | copy-start | bytes 884740
  7.0 10.7 %collective-permute-start.24 = (bf16[128,1152]{1,0:T(8,128)(2,1)S(1)}, bf16[128,1152]{1,0:T(8,128)(2,1)}, u32[]{:S(2)}, u32[]{:S(2)}) collective-permute-start(bf16[128,1152]{1,0:T(8,128)(2,1)S(1)} %param.24), channel_id=1, source_target_pairs={{0,64},{1,65},{2,66},{3,67},{4,68},{5,69},{6,70},{7,71},{8,72},{9,... | collective-permute-start | bytes 884744 | tf_op jit(solution)/shard_map/cond/branch_6_fun/ppermute | solution.py:18
  21.7 9.9 %collective-permute-start.13 = (bf16[128,1152]{1,0:T(8,128)(2,1)S(1)}, bf16[128,1152]{1,0:T(8,128)(2,1)}, u32[]{:S(2)}, u32[]{:S(2)}) collective-permute-start(bf16[128,1152]{1,0:T(8,128)(2,1)S(1)} %param.13), channel_id=1, source_target_pairs={{0,16},{1,17},{2,18},{3,19},{4,20},{5,21},{6,22},{7,23},{8,24},{9,... | collective-permute-start | bytes 884744 | tf_op jit(solution)/shard_map/cond/branch_4_fun/ppermute | solution.py:18
  35.1 15.6 %collective-permute-start.8 = (bf16[128,1152]{1,0:T(8,128)(2,1)S(1)}, bf16[128,1152]{1,0:T(8,128)(2,1)}, u32[]{:S(2)}, u32[]{:S(2)}) collective-permute-start(bf16[128,1152]{1,0:T(8,128)(2,1)S(1)} %param.8), channel_id=1, source_target_pairs={{0,256},{1,257},{2,258},{3,259},{4,260},{5,261},{6,262},{7,263},{8... | collective-permute-start | bytes 884744 | tf_op jit(solution)/shard_map/cond/branch_8_fun/ppermute | solution.py:18
  57.9 14.0 %collective-permute-start.51 = (bf16[128,1152]{1,0:T(8,128)(2,1)S(1)}, bf16[128,1152]{1,0:T(8,128)(2,1)}, u32[]{:S(2)}, u32[]{:S(2)}) collective-permute-start(bf16[128,1152]{1,0:T(8,128)(2,1)S(1)} %param.51), channel_id=1, source_target_pairs={{0,64},{1,65},{2,66},{3,67},{4,68},{5,69},{6,70},{7,71},{8,72},{9,... | collective-permute-start | bytes 884744 | tf_op jit(solution)/shard_map/cond/branch_6_fun/ppermute | solution.py:18
  72.1 10.3 %collective-permute-start.40 = (bf16[128,1152]{1,0:T(8,128)(2,1)S(1)}, bf16[128,1152]{1,0:T(8,128)(2,1)}, u32[]{:S(2)}, u32[]{:S(2)}) collective-permute-start(bf16[128,1152]{1,0:T(8,128)(2,1)S(1)} %param.40), channel_id=1, source_target_pairs={{0,16},{1,17},{2,18},{3,19},{4,20},{5,21},{6,22},{7,23},{8,24},{9,... | collective-permute-start | bytes 884744 | tf_op jit(solution)/shard_map/cond/branch_4_fun/ppermute | solution.py:18
  82.7 18.0 %collective-permute-start.35 = (bf16[128,1152]{1,0:T(8,128)(2,1)S(1)}, bf16[128,1152]{1,0:T(8,128)(2,1)}, u32[]{:S(2)}, u32[]{:S(2)}) collective-permute-start(bf16[128,1152]{1,0:T(8,128)(2,1)S(1)} %param.35), channel_id=1, source_target_pairs={{0,256},{1,257},{2,258},{3,259},{4,260},{5,261},{6,262},{7,263},{8... | collective-permute-start | bytes 884744 | tf_op jit(solution)/shard_map/cond/branch_8_fun/ppermute | solution.py:18
where the time goes:
time: 104 us; the launch traced here: 103 us
  waiting for transfers between devices  48.6 us (47%)
  starting transfers between devices  29.8 us (29%)
  matrix products  10.5 us (10%)
  between operations  6.71 us (6%)
  other arithmetic  6 us (6%)
  local copies, waits for them, and re-layouts  1.47 us (1%)
    ppermute x6, waiting for transfers between devices, partner_2(): return lax.ppermute(value, axis, pairs)  48.6 us
    ppermute x6, starting transfers between devices, partner_2(): return lax.ppermute(value, axis, pairs)  29.8 us
    dot_general x4, matrix products, pair_block(): jnp.dot(coef, txt_block, preferred_element_type=jnp.float32)  4.1 us
    dot_general x4, matrix products, pair_block(): jnp.dot(img_block, txt_block.T, preferred_element_type=jnp.float32)  4.1 us
    dot_general x4, matrix products, text_part(): jnp.einsum('ij,id->jd', coef, img_block, preferred_element_type=jnp.float32)  2.27 us
  transfers between devices with their start and end apart: 6, of which 6 were waited for; matrix products, arithmetic and copies ran while one was open for 0% of the time, Pallas kernels for 0%

commit v1 on v0

v1 whole, which is shorter than its diff:
```python
import functools

import jax
import jax.numpy as jnp
from jax import lax
from jax.experimental import pallas as pl
from jax.experimental.pallas import tpu as pltpu
from jax.sharding import PartitionSpec as P

MESH = pl.DeviceIdType.MESH
ROUNDS = 3
ROWS = 128
BOTH = 2 * ROWS
CHUNKS = 8
SLICE = BOTH // CHUNKS
PIECE = 2 * SLICE
PIECES = BOTH // PIECE
STEPS = 3 * CHUNKS
TOP_BIT = 8
RINGS = ((6, 3), (1, 3), (4, 2))
WINDOWS = tuple((low, high) for high in range(TOP_BIT) for low in range(high))


def div(a, b):
    return lax.div(a, jnp.int32(b))


def rem(a, b):
    return lax.rem(a, jnp.int32(b))


def pick(index, table):
    value = jnp.int32(table[0])
    for k in range(1, len(table)):
        if table[k] != table[k - 1]:
            value = jnp.where(index >= k, jnp.int32(table[k]), value)
    return value


class Direct:
    buffers = 1
    phases = 0
    final = 0

    def __init__(self, bit):
        self.bit = bit

    def place(self, me):
        mask = 1 << self.bit
        self.partner = me + (1 - 2 * rem(div(me, mask), 2)) * mask

    def neighbours(self):
        return [self.partner]

    def first(self, chunk):
        return 0, self.partner


class Relay:
    def __init__(self, ring, kind, hops):
        self.bit, count = ring
        self.size = 1 << count
        self.kind = kind
        self.phases = hops - 1
        self.buffers = 6 if kind == "two" else hops
        self.final = self.buffers - 1

    def place(self, me):
        self.me = me
        self.at = rem(div(me, 1 << self.bit), self.size)
        self.low = rem(div(self.at, 2), 2)
        self.mid = rem(div(self.at + 1, 2), 2)

    def device(self, step):
        return self.me + (rem(self.at + step + self.size, self.size) - self.at) * (1 << self.bit)

    def neighbours(self):
        return [self.device(1), self.device(-1)]

    def first(self, chunk):
        if self.kind == "both":
            return 0, self.device(1 - 2 * rem(chunk, 2))
        if self.kind == "one":
            return 0, self.device(1 - 2 * rem(self.at, 2))
        return self.low, self.device(1 - 2 * self.low)

    def hop(self, phase, chunk):
        if self.kind == "both":
            return phase - 1, phase, self.device(1 - 2 * rem(chunk, 2))
        if self.kind == "one":
            return phase - 1, phase, self.device(1 - 2 * rem(self.at + phase, 2))
        low, mid = self.low, self.mid
        ahead = 1 - 2 * low
        second = phase == 2
        here = jnp.where(
            mid == 1,
            jnp.where(phase == 1, 1 - low, jnp.where(second, low, 2)),
            jnp.where(phase == 1, 2, jnp.where(second, 3 + low, 4 - low)),
        )
        there = jnp.where(mid == 1, jnp.where(phase == 3, 4 - low, 2), jnp.where(phase == 1, 4 - low, 5))
        return here, there, self.device(jnp.where(second, ahead, -ahead))


def routes(bits):
    flows, blocks = [], []

    def direct(bit, how):
        flows.append(Direct(bit))
        blocks.append((flows[-1], 0, how))

    for ring in RINGS:
        first, count = ring
        held = tuple(b - first for b in bits if first <= b < first + count)
        if count == 3 and 2 in held:
            kind = "two" if 1 in held else "one" if 0 in held else "both"
            flow = Relay(ring, kind, 4)
            flows.append(flow)
            blocks.append((flow, flow.final, "last" if first + 2 == TOP_BIT else "late"))
            if kind == "two":
                blocks.append((flow, 2, "passed two"))
                if 0 in held:
                    direct(first, "after")
            elif kind == "one":
                blocks.append((flow, 0, "passed one"))
        elif count == 2 and len(held) == 2:
            flow = Relay(ring, "one", 2)
            flows.append(flow)
            blocks.append((flow, flow.final, "early"))
            blocks.append((flow, 0, "passed one"))
        else:
            for low in held:
                direct(first + low, "late" if count == 3 and 1 in held else "early")
    if 0 in bits:
        direct(0, "early")
    return flows, blocks


def agenda(kind, blocks):
    tasks = [(piece, 0, piece) for piece in range(PIECES)]
    early = 0
    for number, (_, _, how) in enumerate(blocks, 1):
        if how == "last":
            steps = {"both": (24, 24, 24, 24), "one": (20, 21, 22, 23), "two": (19, 21, 23, 24)}[kind]
        elif how == "passed two":
            steps = (17, 19, 21, 23)
        elif how == "passed one":
            steps = (4, 5, 6, 7) if kind == "one" else (9, 10, 11, 12)
        elif how == "early":
            steps = (16, 18, 20, 22) if kind == "two" else tuple(16 + 4 * early + k for k in range(4))
            early += 1
        elif how == "late":
            steps = (24, 24, 24, 24) if kind == "both" else (21, 22, 23, 24)
        else:
            steps = (24, 24, 24, 24)
        tasks += [(step, number, piece) for piece, step in enumerate(steps)]
    after = [how == "after" for _, _, how in blocks]
    tasks.sort(key=lambda t: (t[0], t[1] > 0 and after[t[1] - 1], t[2], -t[1]))
    return tasks


def kernel(bits, img_hbm, txt_hbm, scale_ref, bias_ref, loss_out, img_out, txt_out,
           raw, norms, held, total, losses, load_sem, store_sem, send_sem, recv_sem):
    me = lax.axis_index("dp")
    flows, blocks = routes(bits)
    base = 1
    for number, flow in enumerate(flows):
        flow.place(me)
        flow.base, flow.sends = base, 4 * number
        base += flow.buffers

    loads = [
        pltpu.make_async_copy(src, raw.at[pl.ds(ROWS * k, ROWS)], load_sem.at[k])
        for k, src in enumerate((txt_hbm, img_hbm))
    ]
    for load in loads:
        load.start()
    barrier = pltpu.get_barrier_semaphore()
    greeted = [d for flow in flows for d in flow.neighbours()]
    for device in greeted:
        pl.semaphore_signal(barrier, inc=1, device_id=(device,), device_id_type=MESH)
    for load in loads:
        load.wait()

    def rows(start, count):
        return pl.ds(pl.multiple_of(start, count), count)

    @pl.loop(0, CHUNKS)
    def _(chunk):
        part = rows(chunk * SLICE, SLICE)
        whole = raw[part, :].astype(jnp.float32)
        norm = jnp.sqrt(jnp.sum(whole * whole, axis=-1, keepdims=True) + 1e-06)
        norms[part, :] = norm
        held[0, part, :] = (whole / norm).astype(jnp.bfloat16)
        total[part, :] = jnp.zeros_like(whole)

    losses[...] = jnp.zeros_like(losses)
    pl.semaphore_wait(barrier, len(greeted))

    def copy(here, there, chunk, send, device):
        part = rows(chunk * SLICE, SLICE)
        return pltpu.make_async_remote_copy(
            src_ref=held.at[here, part],
            dst_ref=held.at[there, part],
            send_sem=send_sem.at[send],
            recv_sem=recv_sem.at[there, chunk],
            device_id=(device,),
            device_id_type=MESH,
        )

    def arrived(buffer, chunk):
        copy(0, buffer, chunk, 0, me).wait_recv()

    @pl.loop(0, CHUNKS)
    def _(chunk):
        for flow in flows:
            there, device = flow.first(chunk)
            copy(0, flow.base + there, chunk, flow.sends, device).start()

    scale, bias = scale_ref[0], bias_ref[0]
    far = next(flow for flow, _, how in blocks if how == "last")
    tasks = agenda(far.kind, blocks)
    where = [0] + [flow.base + buffer for flow, buffer, _ in blocks]
    open_ = [0] + [int(not how.startswith("passed")) for _, _, how in blocks]

    def pair(task):
        block = pick(task, [t[1] for t in tasks])
        piece = pick(task, [t[2] for t in tasks])
        buffer = pick(block, where)

        @pl.when(pick(block, open_) == 1)
        def _():
            arrived(buffer, 2 * piece)
            arrived(buffer, 2 * piece + 1)

        side = div(piece, PIECES // 2)
        mine = rows(ROWS - ROWS * side, ROWS)
        other = held[buffer, rows(piece * PIECE, PIECE), :]
        logits = scale * lax.dot_general(
            held[0, mine, :], other, (((1,), (1,)), ((), ())), preferred_element_type=jnp.float32
        ) + bias
        row = lax.broadcasted_iota(jnp.int32, logits.shape, 0)
        column = lax.broadcasted_iota(jnp.int32, logits.shape, 1) + rem(piece, PIECES // 2) * PIECE
        diagonal = row == jnp.where(block == 0, column, -1)
        logits = jnp.where(diagonal, -logits, logits)
        small = jnp.exp(-jnp.abs(logits))
        share = 1.0 / (1.0 + small)
        coef = jnp.where(logits >= 0, share, small * share)
        coef = jnp.where(diagonal, -coef, coef)
        loss = jnp.maximum(logits, 0.0) + jnp.log1p(small)
        losses[:, :PIECE] += jnp.where(side == 0, loss, 0.0)
        total[mine, :] += jnp.dot(coef.astype(jnp.bfloat16), other, preferred_element_type=jnp.float32)

    due = [sum(t[0] < step for t in tasks) for step in range(STEPS + 2)]

    @pl.loop(0, STEPS + 1)
    def _(step):
        phase = div(step, CHUNKS) + 1
        chunk = rem(step, CHUNKS)
        for flow in flows:
            if flow.phases:
                @pl.when(phase <= flow.phases)
                def _(flow=flow):
                    here, there, device = flow.hop(phase, chunk)
                    arrived(flow.base + here, chunk)
                    copy(flow.base + here, flow.base + there, chunk, flow.sends + phase, device).start()

        @pl.loop(pick(step, due), pick(step + 1, due))
        def _(task):
            pair(task)

    @pl.loop(0, CHUNKS)
    def _(chunk):
        part = rows(chunk * SLICE, SLICE)
        direction = scale * total[part, :]
        scaled = 1.0 / norms[part, :]
        unit = raw[part, :].astype(jnp.float32) * scaled
        inner = jnp.sum(unit * direction, axis=-1, keepdims=True)
        total[part, :] = (direction - unit * inner) * scaled

    stores = [
        pltpu.make_async_copy(total.at[pl.ds(ROWS * k, ROWS)], out, store_sem.at[k])
        for k, out in enumerate((txt_out, img_out))
    ]
    for store in stores:
        store.start()
    loss_out[...] = jnp.sum(losses[...].T, axis=0, keepdims=True)
    for flow in flows:
        for phase in range(flow.phases + 1):
            pltpu.make_async_remote_copy(
                src_ref=held.at[0], dst_ref=held.at[flow.base], send_sem=send_sem.at[flow.sends + phase],
                recv_sem=recv_sem.at[flow.base, 0], device_id=(me,), device_id_type=MESH,
            ).wait_send()
    for store in stores:
        store.wait()


def window(number, image, text, scale, bias):
    bits = (*WINDOWS[number], TOP_BIT)
    flows, _ = routes(bits)
    buffers = 1 + sum(flow.buffers for flow in flows)
    width = image.shape[1]
    any_space = pl.BlockSpec(memory_space=pl.ANY)
    scalar = pl.BlockSpec(memory_space=pltpu.SMEM)
    return pl.pallas_call(
        functools.partial(kernel, bits),
        out_shape=(
            jax.ShapeDtypeStruct((1, ROWS), jnp.float32),
            jax.ShapeDtypeStruct((ROWS, width), jnp.float32),
            jax.ShapeDtypeStruct((ROWS, width), jnp.float32),
        ),
        in_specs=[any_space, any_space, scalar, scalar],
        out_specs=(pl.BlockSpec(memory_space=pltpu.VMEM), any_space, any_space),
        scratch_shapes=[
            pltpu.VMEM((BOTH, width), jnp.bfloat16),
            pltpu.VMEM((BOTH, 1), jnp.float32),
            pltpu.VMEM((buffers, BOTH, width), jnp.bfloat16),
            pltpu.VMEM((BOTH, width), jnp.float32),
            pltpu.VMEM((ROWS, ROWS), jnp.float32),
            pltpu.SemaphoreType.DMA((2,)),
            pltpu.SemaphoreType.DMA((2,)),
            pltpu.SemaphoreType.DMA((4 * len(flows),)),
            pltpu.SemaphoreType.DMA((buffers, CHUNKS)),
        ],
        compiler_params=pltpu.CompilerParams(
            collective_id=number, has_side_effects=True, vmem_limit_bytes=24 << 20
        ),
        name="window",
    )(image, text, scale, bias)


def per_device(image, text, plan, offset, logit_scale, logit_bias):
    listed = jnp.arange(plan.shape[0], dtype=jnp.int32) - offset[0]
    others = jnp.sum(jnp.where((listed >= 0) & (listed < ROUNDS), plan[:, 0], 0)) - (1 << TOP_BIT)
    high = 31 - lax.clz(others)
    low = 31 - lax.clz(others - jnp.left_shift(jnp.int32(1), high))
    number = high * (high - 1) // 2 + low
    branches = [functools.partial(window, k) for k in range(len(WINDOWS))]
    losses, image_grad, text_grad = lax.switch(number, branches, image, text, logit_scale, logit_bias)
    return losses.reshape(ROWS), image_grad, text_grad


def solution(mesh):
    in_specs = (P("dp", None), P("dp", None), P(), P(), P(), P())
    out_specs = (P("dp"), P("dp", None), P("dp", None))
    return jax.shard_map(
        per_device, mesh=mesh, in_specs=in_specs, out_specs=out_specs, check_vma=False
    )
```

time: 104 us -> 57.6 us (0.55)
  the two profiles are of different devices: /device:TPU:198 before, /device:TPU:6 now
where the time goes in v1:
time: 57.6 us; the launch traced here: 56.6 us
  Pallas kernels  50.8 us (88%)
  local copies, waits for them, and re-layouts  2.94 us (5%)
  between operations  1.97 us (3%)
  other arithmetic  0.64 us (1%)
    pallas_call x1, Pallas kernels, window(): pl.pallas_call(functools.partial(kernel, bits), out_shape=(jax.ShapeDtype...  50.8 us
    unnamed x3, local copies, waits for them, and re-layouts  2.14 us

profile of v1, /device:TPU:6, one launch (start us, length us, event | category | flops | bytes accessed | tf_op | source)
XLA Modules:
  0.0 56.6 jit_solution(17254502536730106238)
XLA Ops:
  1.3 0.8 %slice_reduce_fusion = s32[5]{0:T(128)S(1)} fusion(s32[5,512]{1,0:T(8,128)} %param.36), kind=kLoop, calls=%fused_computation | loop fusion | bytes 40 | tf_op jit(solution)/shard_map/slice | solution.py:333
  2.1 0.6 %fusion = s32[]{:T(128)} fusion(s32[5]{0:T(128)S(1)} %slice_reduce_fusion, s32[]{:T(128)} %bitcast.29), kind=kLoop, calls=%fused_computation.2 | loop fusion | flops 29 | bytes 28 | tf_op jit(solution)/shard_map/reduce_sum | solution.py:333
  3.4 51.0 %conditional.1 = (f32[128,1152]{1,0:T(8,128)S(1)}, f32[128,1152]{1,0:T(8,128)S(1)}, f32[128]{0:T(128)S(1)}) conditional(s32[]{:T(128)} %clamp.3, (bf16[128,1152]{1,0:T(8,128)(2,1)}, bf16[128,1152]{1,0:T(8,128)(2,1)}, f32[1]{0:T(128)}, f32[1]{0:T(128)}) %tuple.148, (bf16[128,1152]{1,0:T(8,128)(2,1)}, ...), branch_computations={%region_1.2_spmd, %region_2.3_spmd, %region_3.4_spmd, %region_4.5_... | conditional | bytes 24 | solution.py:338
  3.6 50.8 %window.46 = (f32[1,128]{1,0:T(1,128)S(1)}, f32[128,1152]{1,0:T(8,128)S(1)}, f32[128,1152]{1,0:T(8,128)S(1)}) custom-call(bf16[128,1152]{1,0:T(8,128)(2,1)} %get-tuple-element.435.img_hbm, bf16[128,1152]{1,0:T(8,128)(2,1)} %get-tuple-element.436.txt_hbm, f32[1]{0:T(128)} %get-tuple-element.437.scale_ref, f32[1]{0:T(128)} %get-tuple-element.438.bias_ref), custom_call_target="tpu_custom_call" | custom-call | tf_op jit(solution)/shard_map/cond/branch_18_fun/window/pallas_call | solution.py:304
  54.4 0.5 copy.97
  55.0 0.8 %copy.98 = f32[128,1152]{1,0:T(8,128)} copy(f32[128,1152]{1,0:T(8,128)S(1)} %get-tuple-element.602) | data formatting | bytes 1179648
  55.8 0.8 %copy.99 = f32[128,1152]{1,0:T(8,128)} copy(f32[128,1152]{1,0:T(8,128)S(1)} %get-tuple-element.603) | data formatting | bytes 1179648

commit v2 on v1

v2 whole, which is shorter than its diff:
```python
import functools

import jax
import jax.numpy as jnp
from jax import lax
from jax.experimental import pallas as pl
from jax.experimental.pallas import tpu as pltpu
from jax.sharding import PartitionSpec as P

MESH = pl.DeviceIdType.MESH
ROUNDS = 3
ROWS = 128
BOTH = 2 * ROWS
CHUNKS = 8
SLICE = BOTH // CHUNKS
PIECE = ROWS
PIECES = BOTH // PIECE
HALF = CHUNKS // 2
STEPS = 3 * CHUNKS
TOP_BIT = 8
RINGS = ((6, 3), (1, 3), (4, 2))
WINDOWS = tuple((low, high) for high in range(TOP_BIT) for low in range(high))


def div(a, b):
    return lax.div(a, jnp.int32(b))


def rem(a, b):
    return lax.rem(a, jnp.int32(b))


def pick(index, table):
    value = jnp.int32(table[0])
    for k in range(1, len(table)):
        if table[k] != table[k - 1]:
            value = jnp.where(index >= k, jnp.int32(table[k]), value)
    return value


class Direct:
    buffers = 1
    phases = 0
    final = 0

    def __init__(self, bit):
        self.bit = bit

    def place(self, me):
        mask = 1 << self.bit
        self.partner = me + (1 - 2 * rem(div(me, mask), 2)) * mask

    def neighbours(self):
        return [self.partner]

    def first(self, chunk):
        return 0, self.partner


class Relay:
    size = 8
    phases = 3
    final = 3

    def __init__(self, bit, taps):
        self.bit = bit
        self.taps = taps
        self.buffers = 4 + len(taps)

    def place(self, me):
        self.me = me
        self.at = rem(div(me, 1 << self.bit), self.size)

    def device(self, step):
        return self.me + (rem(self.at + step + self.size, self.size) - self.at) * (1 << self.bit)

    def side(self, tap):
        return rem(div(self.at, 1 << tap), 2)

    def partner(self, tap):
        return self.me + (1 - 2 * self.side(tap)) * (1 << (self.bit + tap))

    def neighbours(self):
        return [self.device(1), self.device(-1)] + [self.partner(tap) for tap in self.taps if tap]

    def slot(self, hop, down, at):
        buffer = hop - 1
        for number, tap in enumerate(self.taps):
            other = (hop == 1 << tap) & (down == rem(div(at, 1 << tap), 2))
            buffer = jnp.where(other, 4 + number, buffer)
        return buffer

    def hop(self, phase, chunk):
        down = rem(chunk, 2)
        step = 1 - 2 * down
        there = rem(self.at + step + self.size, self.size)
        return self.slot(phase, down, self.at), self.slot(phase + 1, down, there), self.device(step)

    def first(self, chunk):
        _, there, device = self.hop(0, chunk)
        return there, device


def routes(bits):
    flows, blocks = [], []

    def direct(bit, how):
        flows.append(Direct(bit))
        blocks.append((flows[-1], 0, how))

    for first, count in RINGS:
        held = tuple(b - first for b in bits if first <= b < first + count)
        if count == 3 and 2 in held:
            flow = Relay(first, held[:-1])
            flows.append(flow)
            blocks.append((flow, flow.final, "last" if first + 2 == TOP_BIT else "late"))
            for tap in flow.taps:
                blocks.append((flow, (1 << tap) - 1, ("near", "far")[tap]))
        else:
            for low in held:
                direct(first + low, "late" if 1 in held and (count == 3 or len(held) == 2) else "early")
    if 0 in bits:
        direct(0, "early")
    return flows, blocks


def agenda(blocks):
    tasks = [(1 + 2 * piece, 0, piece) for piece in range(PIECES)]
    early = 0
    for number, (flow, _, how) in enumerate(blocks, 1):
        if how in ("early", "near"):
            steps = (16 + 4 * early, 18 + 4 * early)
            early += 1
        else:
            steps = (24 if flow.phases else 22, 24)
        tasks += [(step, number, piece) for piece, step in enumerate(steps)]
    tasks.sort(key=lambda t: (t[0], t[2], -t[1]))
    return tasks


def kernel(bits, img_hbm, txt_hbm, scale_ref, bias_ref, loss_out, img_out, txt_out,
           raw, norms, held, total, losses, load_sem, store_sem, send_sem, recv_sem):
    me = lax.axis_index("dp")
    flows, blocks = routes(bits)
    base = 1
    for number, flow in enumerate(flows):
        flow.place(me)
        flow.base, flow.sends = base, 6 * number
        base += flow.buffers

    loads = [
        pltpu.make_async_copy(src, raw.at[pl.ds(ROWS * k, ROWS)], load_sem.at[k])
        for k, src in enumerate((txt_hbm, img_hbm))
    ]
    for load in loads:
        load.start()
    barrier = pltpu.get_barrier_semaphore()
    greeted = [d for flow in flows for d in flow.neighbours()]
    for device in greeted:
        pl.semaphore_signal(barrier, inc=1, device_id=(device,), device_id_type=MESH)
    for load in loads:
        load.wait()

    def rows(start, count):
        return pl.ds(pl.multiple_of(start, count), count)

    def copy(here, there, chunk, send, device):
        part = rows(chunk * SLICE, SLICE)
        return pltpu.make_async_remote_copy(
            src_ref=held.at[here, part],
            dst_ref=held.at[there, part],
            send_sem=send_sem.at[send],
            recv_sem=recv_sem.at[there, chunk],
            device_id=(device,),
            device_id_type=MESH,
        )

    def arrived(buffer, chunk):
        copy(0, buffer, chunk, 0, me).wait_recv()

    pl.semaphore_wait(barrier, len(greeted))

    @pl.loop(0, CHUNKS)
    def _(chunk):
        part = rows(chunk * SLICE, SLICE)
        whole = raw[part, :].astype(jnp.float32)
        norm = jnp.sqrt(jnp.sum(whole * whole, axis=-1, keepdims=True) + 1e-06)
        norms[part, :] = norm
        held[0, part, :] = (whole / norm).astype(jnp.bfloat16)
        for flow in flows:
            there, device = flow.first(chunk)
            copy(0, flow.base + there, chunk, flow.sends, device).start()

    for flow in flows:
        for number, tap in enumerate(getattr(flow, "taps", ())):
            @pl.loop(0, CHUNKS // 2)
            def _(pair, flow=flow, number=number, tap=tap):
                copy(0, flow.base + (1 << tap) - 1, 2 * pair + 1 - flow.side(tap), flow.sends + 4 + number,
                     flow.partner(tap)).start()

    total[...] = jnp.zeros_like(total)
    losses[...] = jnp.zeros_like(losses)

    scale, bias = scale_ref[0], bias_ref[0]
    tasks = agenda(blocks)
    ends = [max(k for k, t in enumerate(tasks) if t[2] == side) for side in range(2)]
    stores = {
        k: pltpu.make_async_copy(total.at[pl.ds(ROWS * k, ROWS)], out, store_sem.at[k])
        for k, out in enumerate((txt_out, img_out))
    }
    where = [0] + [flow.base + buffer for flow, buffer, _ in blocks]
    waits = [0] + [2 if how in ("near", "far") else 1 for _, _, how in blocks]

    def finish(side):
        @pl.loop(0, CHUNKS // 2)
        def _(chunk):
            part = rows(ROWS - ROWS * side + chunk * SLICE, SLICE)
            direction = scale * total[part, :]
            scaled = 1.0 / norms[part, :]
            unit = raw[part, :].astype(jnp.float32) * scaled
            inner = jnp.sum(unit * direction, axis=-1, keepdims=True)
            total[part, :] = (direction - unit * inner) * scaled

        for k, store in stores.items():
            @pl.when(side == 1 - k)
            def _(store=store):
                store.start()

    def pair(task):
        block = pick(task, [t[1] for t in tasks])
        piece = pick(task, [t[2] for t in tasks])
        buffer = pick(block, where)

        @pl.when(pick(block, waits) == 1)
        def _():
            for chunk in range(HALF):
                arrived(buffer, HALF * piece + chunk)

        for number, (flow, _, how) in enumerate(blocks, 1):
            if waits[number] == 2:
                @pl.when(block == number)
                def _(flow=flow, tap=("near", "far").index(how)):
                    for chunk in range(0, HALF, 2):
                        arrived(buffer, HALF * piece + chunk + flow.side(tap))

        side = piece
        mine = rows(ROWS - ROWS * side, ROWS)
        other = held[buffer, rows(piece * PIECE, PIECE), :]
        logits = scale * lax.dot_general(
            held[0, mine, :], other, (((1,), (1,)), ((), ())), preferred_element_type=jnp.float32
        ) + bias
        row = lax.broadcasted_iota(jnp.int32, logits.shape, 0)
        column = lax.broadcasted_iota(jnp.int32, logits.shape, 1)
        diagonal = row == jnp.where(block == 0, column, -1)
        logits = jnp.where(diagonal, -logits, logits)
        small = jnp.exp(-jnp.abs(logits))
        share = 1.0 / (1.0 + small)
        coef = jnp.where(logits >= 0, share, small * share)
        coef = jnp.where(diagonal, -coef, coef)
        loss = jnp.maximum(logits, 0.0) + jnp.log1p(small)
        losses[...] += jnp.where(side == 0, loss, 0.0)
        total[mine, :] += jnp.dot(coef.astype(jnp.bfloat16), other, preferred_element_type=jnp.float32)

        @pl.when((task == ends[0]) | (task == ends[1]))
        def _():
            finish(side)

    due = [sum(t[0] < step for t in tasks) for step in range(STEPS + 2)]

    @pl.loop(0, STEPS + 1)
    def _(step):
        phase = div(step, CHUNKS) + 1
        chunk = rem(step, CHUNKS)
        for flow in flows:
            if flow.phases:
                @pl.when(phase <= flow.phases)
                def _(flow=flow):
                    here, there, device = flow.hop(phase, chunk)
                    arrived(flow.base + here, chunk)
                    copy(flow.base + here, flow.base + there, chunk, flow.sends + phase, device).start()

        @pl.loop(pick(step, due), pick(step + 1, due))
        def _(task):
            pair(task)

    loss_out[...] = jnp.sum(losses[...].T, axis=0, keepdims=True)
    for flow in flows:
        for phase in range(flow.phases + 1):
            pltpu.make_async_remote_copy(
                src_ref=held.at[0], dst_ref=held.at[flow.base], send_sem=send_sem.at[flow.sends + phase],
                recv_sem=recv_sem.at[flow.base, 0], device_id=(me,), device_id_type=MESH,
            ).wait_send()
        for number in range(len(getattr(flow, "taps", ()))):
            pltpu.make_async_remote_copy(
                src_ref=held.at[0, pl.ds(0, ROWS)], dst_ref=held.at[flow.base, pl.ds(0, ROWS)],
                send_sem=send_sem.at[flow.sends + 4 + number], recv_sem=recv_sem.at[flow.base, 0],
                device_id=(me,), device_id_type=MESH,
            ).wait_send()
    for store in stores.values():
        store.wait()


def hand_over(*refs):
    count = (len(refs) - 1) // 2
    copies = [pltpu.make_async_copy(refs[k], refs[count + k], refs[-1].at[k]) for k in range(count)]
    for copy in copies:
        copy.start()
    for copy in copies:
        copy.wait()


def moved(arrays):
    return pl.pallas_call(
        hand_over,
        out_shape=tuple(jax.ShapeDtypeStruct(a.shape, a.dtype) for a in arrays),
        in_specs=[pl.BlockSpec(memory_space=pl.ANY)] * len(arrays),
        out_specs=tuple(pl.BlockSpec(memory_space=pl.ANY) for _ in arrays),
        scratch_shapes=[pltpu.SemaphoreType.DMA((len(arrays),))],
        name="moved",
    )(*arrays)


def window(number, image, text, scale, bias):
    bits = (*WINDOWS[number], TOP_BIT)
    flows, _ = routes(bits)
    buffers = 1 + sum(flow.buffers for flow in flows)
    width = image.shape[1]
    any_space = pl.BlockSpec(memory_space=pl.ANY)
    scalar = pl.BlockSpec(memory_space=pltpu.SMEM)
    return pl.pallas_call(
        functools.partial(kernel, bits),
        out_shape=(
            jax.ShapeDtypeStruct((1, ROWS), jnp.float32),
            jax.ShapeDtypeStruct((ROWS, width), jnp.float32),
            jax.ShapeDtypeStruct((ROWS, width), jnp.float32),
        ),
        in_specs=[any_space, any_space, scalar, scalar],
        out_specs=(pl.BlockSpec(memory_space=pltpu.VMEM), any_space, any_space),
        scratch_shapes=[
            pltpu.VMEM((BOTH, width), jnp.bfloat16),
            pltpu.VMEM((BOTH, 1), jnp.float32),
            pltpu.VMEM((buffers, BOTH, width), jnp.bfloat16),
            pltpu.VMEM((BOTH, width), jnp.float32),
            pltpu.VMEM((ROWS, ROWS), jnp.float32),
            pltpu.SemaphoreType.DMA((2,)),
            pltpu.SemaphoreType.DMA((2,)),
            pltpu.SemaphoreType.DMA((6 * len(flows),)),
            pltpu.SemaphoreType.DMA((buffers, CHUNKS)),
        ],
        compiler_params=pltpu.CompilerParams(
            collective_id=number, has_side_effects=True, vmem_limit_bytes=24 << 20
        ),
        name="window",
    )(image, text, scale, bias)


def per_device(image, text, plan, offset, logit_scale, logit_bias):
    listed = jnp.arange(plan.shape[0], dtype=jnp.int32) - offset[0]
    others = jnp.sum(jnp.where((listed >= 0) & (listed < ROUNDS), plan[:, 0], 0)) - (1 << TOP_BIT)
    high = 31 - lax.clz(others)
    low = 31 - lax.clz(others - jnp.left_shift(jnp.int32(1), high))
    number = lax.shift_right_logical(high * (high - 1), jnp.int32(1)) + low
    branches = [functools.partial(window, k) for k in range(len(WINDOWS))]
    results = lax.switch(number, branches, image, text, logit_scale, logit_bias)
    losses, image_grad, text_grad = moved(results)
    return losses.reshape(ROWS), image_grad, text_grad


def solution(mesh):
    in_specs = (P("dp", None), P("dp", None), P(), P(), P(), P())
    out_specs = (P("dp"), P("dp", None), P("dp", None))
    return jax.shard_map(
        per_device, mesh=mesh, in_specs=in_specs, out_specs=out_specs, check_vma=False
    )
```

time: 57.6 us -> 48.4 us (0.84); the launches traced: 56.6 us -> 48.2 us
  Pallas kernels: 50.8 us -> 44.4 us
  local copies, waits for them, and re-layouts: 2.94 us -> 0.8 us
    pallas_call x1, Pallas kernels: 50.8 us -> 43.4 us  [window(): pl.pallas_call(functools.partial(kernel, bits), out_shape=(jax.ShapeDtype...]
    unnamed x3 -> x0, local copies, waits for them, and re-layouts: 2.14 us -> none
    pallas_call x0 -> x1, Pallas kernels: none -> 1.04 us  [moved(): pl.pallas_call(hand_over, out_shape=tuple((jax.ShapeDtypeStruct(a.shape,...]
where the time goes in v2:
time: 48.4 us; the launch traced here: 48.2 us
  Pallas kernels  44.4 us (92%)
  between operations  2.11 us (4%)
  local copies, waits for them, and re-layouts  0.8 us (2%)
  other arithmetic  0.64 us (1%)
    pallas_call x1, Pallas kernels, window(): pl.pallas_call(functools.partial(kernel, bits), out_shape=(jax.ShapeDtype...  43.4 us
    pallas_call x1, Pallas kernels, moved(): pl.pallas_call(hand_over, out_shape=tuple((jax.ShapeDtypeStruct(a.shape,...  1.04 us

profile of v2, /device:TPU:6, one launch (start us, length us, event | category | flops | bytes accessed | tf_op | source)
XLA Modules:
  0.0 48.2 jit_solution(727007832781490848)
XLA Ops:
  1.3 0.8 %slice_reduce_fusion = s32[5]{0:T(128)S(1)} fusion(s32[5,512]{1,0:T(8,128)} %param.36), kind=kLoop, calls=%fused_computation | loop fusion | bytes 40 | tf_op jit(solution)/shard_map/slice | solution.py:359
  2.1 0.6 %fusion = s32[]{:T(128)} fusion(s32[5]{0:T(128)S(1)} %slice_reduce_fusion, s32[]{:T(128)} %bitcast.2), kind=kLoop, calls=%fused_computation.2 | loop fusion | flops 29 | bytes 28 | tf_op jit(solution)/shard_map/reduce_sum | solution.py:359
  3.4 43.7 %conditional.1 = ((f32[1,128]{1,0:T(1,128)S(1)}, f32[128,1152]{1,0:T(8,128)S(1)}, f32[128,1152]{1,0:T(8,128)S(1)})) conditional(s32[]{:T(128)} %clamp.3, (bf16[128,1152]{1,0:T(8,128)(2,1)}, bf16[128,1152]{1,0:T(8,128)(2,1)}, f32[1]{0:T(128)}, f32[1]{0:T(128)}) %tuple.92, (bf16[128,1152]{1,0:T(8,128)(2,1)}, ...), branch_computations={%region_1.2_spmd, %region_2.3_spmd, %region_3.4_spmd, %region_4.5_... | conditional | bytes 8 | solution.py:364
  3.4 43.4 %window.37 = (f32[1,128]{1,0:T(1,128)S(1)}, f32[128,1152]{1,0:T(8,128)S(1)}, f32[128,1152]{1,0:T(8,128)S(1)}) custom-call(bf16[128,1152]{1,0:T(8,128)(2,1)} %get-tuple-element.260.img_hbm, bf16[128,1152]{1,0:T(8,128)(2,1)} %get-tuple-element.261.txt_hbm, f32[1]{0:T(128)} %get-tuple-element.262.scale_ref, f32[1]{0:T(128)} %get-tuple-element.263.bias_ref), custom_call_target="tpu_custom_call" | custom-call | tf_op jit(solution)/shard_map/cond/branch_9_fun/window/pallas_call | solution.py:330
  47.0 1.0 %moved.1 = (f32[1,128]{1,0:T(1,128)}, f32[128,1152]{1,0:T(8,128)}, f32[128,1152]{1,0:T(8,128)}) custom-call(f32[1,128]{1,0:T(1,128)S(1)} %get-tuple-element.345.refs_0_, f32[128,1152]{1,0:T(8,128)S(1)} %get-tuple-element.346.refs_1_, f32[128,1152]{1,0:T(8,128)S(1)} %get-tuple-element.347.refs_2_), custom_call_target="tpu_custom_call" | custom-call | tf_op jit(solution)/shard_map/moved/pallas_call | solution.py:313

commit v3 on v2

--- a/solution.py
+++ b/solution.py
@@ -128,18 +128,26 @@
     tasks = [(1 + 2 * piece, 0, piece) for piece in range(PIECES)]
     early = 0
     for number, (flow, _, how) in enumerate(blocks, 1):
-        if how in ("early", "near"):
+        if how == "early":
             steps = (16 + 4 * early, 18 + 4 * early)
             early += 1
         else:
             steps = (24 if flow.phases else 22, 24)
         tasks += [(step, number, piece) for piece, step in enumerate(steps)]
-    tasks.sort(key=lambda t: (t[0], t[2], -t[1]))
-    return tasks
+    order = ("near", "late", "far", "last")
+
+    def key(task):
+        step, block, piece = task
+        if step < STEPS:
+            return step, piece, 0
+        how = blocks[block - 1][2]
+        return step, piece if how in ("late", "last") else 0, order.index(how)
+
+    return sorted(tasks, key=key)
 
 
 def kernel(bits, img_hbm, txt_hbm, scale_ref, bias_ref, loss_out, img_out, txt_out,
-           raw, norms, held, total, losses, load_sem, store_sem, send_sem, recv_sem):
+           raw, norms, held, total, losses, load_sem, store_sem, send_sem, recv_sem, ready_sem):
     me = lax.axis_index("dp")
     flows, blocks = routes(bits)
     base = 1
@@ -156,8 +164,14 @@
         load.start()
     barrier = pltpu.get_barrier_semaphore()
     greeted = [d for flow in flows for d in flow.neighbours()]
+    far = next(flow for flow, _, how in blocks if how == "last")
+    early_edge = (far.at == 0) | (far.at == 3)
+    late_edge = (far.at == 4) | (far.at == 7)
+    over = far.device(jnp.where((far.at == 0) | (far.at == 4), -1, 1))
     for device in greeted:
-        pl.semaphore_signal(barrier, inc=1, device_id=(device,), device_id_type=MESH)
+        @pl.when(jnp.logical_not(late_edge & (device == over)))
+        def _(device=device):
+            pl.semaphore_signal(barrier, inc=1, device_id=(device,), device_id_type=MESH)
     for load in loads:
         load.wait()
 
@@ -178,7 +192,11 @@
     def arrived(buffer, chunk):
         copy(0, buffer, chunk, 0, me).wait_recv()
 
-    pl.semaphore_wait(barrier, len(greeted))
+    pl.semaphore_wait(barrier, len(greeted) - early_edge.astype(jnp.int32))
+
+    @pl.when(late_edge)
+    def _():
+        pl.semaphore_signal(ready_sem, inc=1, device_id=(over,), device_id_type=MESH)
 
     @pl.loop(0, CHUNKS)
     def _(chunk):
@@ -189,14 +207,40 @@
         held[0, part, :] = (whole / norm).astype(jnp.bfloat16)
         for flow in flows:
             there, device = flow.first(chunk)
-            copy(0, flow.base + there, chunk, flow.sends, device).start()
-
+            if flow is far:
+                @pl.when(jnp.logical_not(early_edge & (device == over)))
+                def _(there=there, device=device):
+                    copy(0, far.base + there, chunk, far.sends, device).start()
+            else:
+                copy(0, flow.base + there, chunk, flow.sends, device).start()
+
+    def send_rest(flow):
+        @pl.loop(0, HALF)
+        def _(two):
+            for number, tap in enumerate(flow.taps):
+                copy(0, flow.base + (1 << tap) - 1, 2 * two + 1 - flow.side(tap), flow.sends + 4 + number,
+                     flow.partner(tap)).start()
+
+    put_off = far.taps == (0,)
+    soon = far.at < 4
     for flow in flows:
-        for number, tap in enumerate(getattr(flow, "taps", ())):
-            @pl.loop(0, CHUNKS // 2)
-            def _(pair, flow=flow, number=number, tap=tap):
-                copy(0, flow.base + (1 << tap) - 1, 2 * pair + 1 - flow.side(tap), flow.sends + 4 + number,
-                     flow.partner(tap)).start()
+        if flow.phases and flow.taps:
+            if flow is far and put_off:
+                @pl.when(soon)
+                def _():
+                    send_rest(far)
+            else:
+                send_rest(flow)
+
+    @pl.when(early_edge)
+    def _():
+        pl.semaphore_wait(ready_sem, 1)
+
+        @pl.loop(0, HALF)
+        def _(two):
+            chunk = 2 * two + (far.at == 0).astype(jnp.int32)
+            there, _ = far.first(chunk)
+            copy(0, far.base + there, chunk, far.sends, over).start()
 
     total[...] = jnp.zeros_like(total)
     losses[...] = jnp.zeros_like(losses)
@@ -278,6 +322,11 @@
                     here, there, device = flow.hop(phase, chunk)
                     arrived(flow.base + here, chunk)
                     copy(flow.base + here, flow.base + there, chunk, flow.sends + phase, device).start()
+
+        if put_off:
+            @pl.when((step == STEPS - 1) & jnp.logical_not(soon))
+            def _():
+                send_rest(far)
 
         @pl.loop(pick(step, due), pick(step + 1, due))
         def _(task):
@@ -346,6 +395,7 @@
             pltpu.SemaphoreType.DMA((2,)),
             pltpu.SemaphoreType.DMA((6 * len(flows),)),
             pltpu.SemaphoreType.DMA((buffers, CHUNKS)),
+            pltpu.SemaphoreType.REGULAR,
         ],
         compiler_params=pltpu.CompilerParams(
             collective_id=number, has_side_effects=True, vmem_limit_bytes=24 << 20

time: 48.4 us -> 54.2 us (1.12)
  Pallas kernels: 44.4 us -> 50.1 us
    pallas_call x1, Pallas kernels: 43.4 us -> 49.1 us  [window(): pl.pallas_call(functools.partial(kernel, bits), out_shape=(jax.ShapeDtype...]
where the time goes in v3:
time: 54.2 us; the launch traced here: 53.9 us
  Pallas kernels  50.1 us (92%)
  between operations  2.11 us (4%)
  local copies, waits for them, and re-layouts  0.8 us (1%)
  other arithmetic  0.64 us (1%)
    pallas_call x1, Pallas kernels, window(): pl.pallas_call(functools.partial(kernel, bits), out_shape=(jax.ShapeDtype...  49.1 us

profile of v3, /device:TPU:6, one launch (start us, length us, event | category | flops | bytes accessed | tf_op | source)
XLA Modules:
  0.0 53.9 jit_solution(6722406737856324672)
XLA Ops:
  1.3 0.8 %slice_reduce_fusion = s32[5]{0:T(128)S(1)} fusion(s32[5,512]{1,0:T(8,128)} %param.36), kind=kLoop, calls=%fused_computation | loop fusion | bytes 40 | tf_op jit(solution)/shard_map/slice | solution.py:409
  2.1 0.6 %fusion = s32[]{:T(128)} fusion(s32[5]{0:T(128)S(1)} %slice_reduce_fusion, s32[]{:T(128)} %bitcast.2), kind=kLoop, calls=%fused_computation.2 | loop fusion | flops 29 | bytes 28 | tf_op jit(solution)/shard_map/reduce_sum | solution.py:409
  3.4 49.4 %conditional.1 = ((f32[1,128]{1,0:T(1,128)S(1)}, f32[128,1152]{1,0:T(8,128)S(1)}, f32[128,1152]{1,0:T(8,128)S(1)})) conditional(s32[]{:T(128)} %clamp.3, (bf16[128,1152]{1,0:T(8,128)(2,1)}, bf16[128,1152]{1,0:T(8,128)(2,1)}, f32[1]{0:T(128)}, f32[1]{0:T(128)}) %tuple.92, (bf16[128,1152]{1,0:T(8,128)(2,1)}, ...), branch_computations={%region_1.2_spmd, %region_2.3_spmd, %region_3.4_spmd, %region_4.5_... | conditional | bytes 8 | solution.py:414
  3.6 49.1 %window.51 = (f32[1,128]{1,0:T(1,128)S(1)}, f32[128,1152]{1,0:T(8,128)S(1)}, f32[128,1152]{1,0:T(8,128)S(1)}) custom-call(bf16[128,1152]{1,0:T(8,128)(2,1)} %get-tuple-element.316.img_hbm, bf16[128,1152]{1,0:T(8,128)(2,1)} %get-tuple-element.317.txt_hbm, f32[1]{0:T(128)} %get-tuple-element.318.scale_ref, f32[1]{0:T(128)} %get-tuple-element.319.bias_ref), custom_call_target="tpu_custom_call" | custom-call | tf_op jit(solution)/shard_map/cond/branch_23_fun/window/pallas_call | solution.py:379
  52.7 1.0 %moved.1 = (f32[1,128]{1,0:T(1,128)}, f32[128,1152]{1,0:T(8,128)}, f32[128,1152]{1,0:T(8,128)}) custom-call(f32[1,128]{1,0:T(1,128)S(1)} %get-tuple-element.345.refs_0_, f32[128,1152]{1,0:T(8,128)S(1)} %get-tuple-element.346.refs_1_, f32[128,1152]{1,0:T(8,128)S(1)} %get-tuple-element.347.refs_2_), custom_call_target="tpu_custom_call" | custom-call | tf_op jit(solution)/shard_map/moved/pallas_call | solution.py:362
